TPU v7x, 512 devices: a whole 4x4x16 slice. The times are simulated.
512 devices in a mesh: row: 16 (over y, x_lo, core), col: 16 (over z), rep: 2 (over x_hi).
Axes of the slice: x: 4 (x_hi: 2, x_lo: 2; x = x_hi * 2 + x_lo), y: 4, z: 16, core: 2. Of those that a mesh axis runs over, the one named last changes fastest.
Arguments:
- layer_inputs: bfloat16 [2, 2048, 6144], P('rep', 'col', 'row'), may hold values from -14 to 14
- output_grads: bfloat16 [2, 2048, 24576], P('rep', 'row', 'col'), may hold values from -0.30935922 to 0.30935922
- error_prev: bfloat16 [2, 6144, 24576], P('rep', 'row', 'col'), may hold values from -72 to 72
- basis_prev: bfloat16 [24576, 64], P('col'), may hold values from -6 to 6
Outputs:
- basis_next: float32 [24576, 64], P('col')
- error_next: bfloat16 [2, 6144, 24576], P('rep', 'row', 'col')
All inputs are finite; a program needn't handle non-finite values.
Results may differ from a plain program's by a relative error of at most 0.005.
Values may be sent and summed in bfloat16 or wider, within the bound.
A program may use at most 64 MiB of HBM per device.

v0:
```python
import jax
import jax.numpy as jnp
from jax import lax
from jax.sharding import PartitionSpec as P


def contract_first(left, right):
    return lax.dot_general(
        left, right, (((0,), (0,)), ((), ())), preferred_element_type=jnp.float32
    )


def body(layer_inputs, output_grads, error_prev, basis_prev):
    replicas = lax.axis_size("rep")
    whole_inputs = lax.all_gather(layer_inputs[0], "col", axis=0, tiled=True)
    whole_grads = lax.all_gather(output_grads[0], "row", axis=0, tiled=True)
    gradient = contract_first(whole_inputs, whole_grads)
    compensated = (gradient + error_prev[0].astype(jnp.float32)).astype(jnp.bfloat16)
    p_local = jnp.dot(compensated, basis_prev, preferred_element_type=jnp.float32)
    projected = lax.psum(p_local, ("col", "rep")) / replicas
    gram_local = lax.dot_general(
        projected,
        projected,
        (((0,), (0,)), ((), ())),
        precision=lax.Precision.HIGHEST,
        preferred_element_type=jnp.float32,
    )
    gram_matrix = lax.psum(gram_local, "row")
    factor = jnp.linalg.cholesky(gram_matrix)
    ortho = lax.linalg.triangular_solve(
        factor, projected, left_side=False, lower=True, transpose_a=True
    )
    ortho_low = ortho.astype(jnp.bfloat16)
    right_local = contract_first(compensated, ortho_low)
    basis_next = lax.psum(right_local, ("row", "rep")) / replicas
    basis_low = basis_next.astype(jnp.bfloat16)
    approx = lax.dot_general(
        ortho_low, basis_low, (((1,), (1,)), ((), ())), preferred_element_type=jnp.float32
    )
    error_next = (compensated.astype(jnp.float32) - approx).astype(jnp.bfloat16)
    return (basis_next, error_next[None])


def solution(mesh):
    return jax.shard_map(
        body,
        mesh=mesh,
        in_specs=(
            P("rep", "col", "row"),
            P("rep", "row", "col"),
            P("rep", "row", "col"),
            P("col", None),
        ),
        out_specs=(P("col", None), P("rep", "row", "col")),
        check_vma=False,
    )
```

profile of v0, /device:TPU:1, one launch (start us, length us, event | category | flops | bytes accessed | tf_op | source)
XLA Modules:
  0.0 644.2 jit_solution(16346551894573752010)
XLA Ops:
  7.2 0.0 all-gather.5.cloned.1.call-start
  7.2 0.7 all-gather.5.cloned.1.call-update
  7.9 0.0 all-gather.7.cloned.1.call-start
  8.0 0.7 all-gather.7.cloned.1.call-update
  8.7 0.0 all-reduce.3.cloned.1.call-start
  8.7 69.3 %all-gather.5.cloned.1.call-done = bf16[1,2048,384]{2,1,0:T(8,128)(2,1)} async-done(((bf16[1,128,384]{2,1,0:T(8,128)(2,1)}), bf16[1,2048,384]{2,1,0:T(8,128)(2,1)}) %all-gather.5.cloned.1.call-update) | async-done | bytes 1572880 | tf_op jit(solution)/shard_map/all_gather | solution.py:15
  78.0 59.2 %all-gather.7.cloned.1.call-done = bf16[1,2048,1536]{2,1,0:T(8,128)(2,1)} async-done(((bf16[1,128,1536]{2,1,0:T(8,128)(2,1)}), bf16[1,2048,1536]{2,1,0:T(8,128)(2,1)}) %all-gather.7.cloned.1.call-update) | async-done | bytes 6291472 | tf_op jit(solution)/shard_map/all_gather | solution.py:16
  137.2 6.2 fusion.5
  143.4 1.2 fusion.22
  144.6 0.0 all-reduce.3.cloned.1.call-update
  144.6 0.0 all-reduce.5.cloned.1.call-start
  144.6 274.5 %all-reduce.3.cloned.1.call-done = f32[384,64]{0,1:T(8,128)} async-done(((f32[384,64]{0,1:T(8,128)}), f32[384,64]{0,1:T(8,128)}) %all-reduce.3.cloned.1.call-update) | async-done | bytes 98320 | tf_op jit(solution)/shard_map/psum | solution.py:20
  419.2 1.2 fusion.13
  420.4 73.0 %psum.22 = f32[64,64]{0,1:T(8,128)S(1)} all-reduce(f32[64,64]{0,1:T(8,128)S(1)} %fusion.13), channel_id=1, replica_groups=mesh['row'=16,'col'=16,'rep'=2] {'row'}, use_global_device_ids=true, to_apply=%region_1.0 | all-reduce | flops 4096 | bytes 32768 | tf_op jit(solution)/shard_map/psum | solution.py:28
  493.4 0.1 copy.7
  493.5 5.8 cholesky.16
  499.4 0.6 compare_reduce_fusion
  500.1 0.7 fusion.17
  500.7 4.9 custom-call.6
  505.6 1.2 convolution_convert_fusion
  506.8 1.1 fusion.23
  507.9 127.2 %all-reduce.5.cloned.1.call-done = f32[1536,64]{0,1:T(8,128)} async-done(((f32[1536,64]{0,1:T(8,128)}), f32[1536,64]{0,1:T(8,128)}) %all-reduce.5.cloned.1.call-update) | async-done | bytes 393232 | tf_op jit(solution)/shard_map/psum | solution.py:35
  635.1 1.0 broadcast_multiply_fusion
  636.1 1.5 fusion.9
  (7 shorter events, 0.1 us)
Async XLA Ops:
  7.2 136.2 %copy-start = (bf16[1536,64]{0,1:T(8,128)(2,1)S(1)}, bf16[1536,64]{0,1:T(8,128)(2,1)}, u32[]{:S(2)}) copy-start(bf16[1536,64]{0,1:T(8,128)(2,1)} %param.7) | copy-start | bytes 589828
  7.2 70.9 %all-gather.5.cloned.1.call-start = ((), (), s32[]{:S(2)}) async-start(), calls=%async_computation.2 | async-start | bytes 1671168 | tf_op jit(solution)/shard_map/all_gather | solution.py:15
  7.9 129.3 %all-gather.7.cloned.1.call-start = ((), (), s32[]{:S(2)}) async-start(), calls=%async_computation.3 | async-start | bytes 6684672 | tf_op jit(solution)/shard_map/all_gather | solution.py:16
  8.7 410.5 %all-reduce.3.cloned.1.call-start = ((), (), s32[]{:S(2)}) async-start(), calls=%async_computation | async-start | bytes 196608 | tf_op jit(solution)/shard_map/psum | solution.py:20
  144.6 490.5 %all-reduce.5.cloned.1.call-start = ((), (), s32[]{:S(2)}) async-start(), calls=%async_computation.1 | async-start | bytes 786432 | tf_op jit(solution)/shard_map/psum | solution.py:35
  636.1 1.5 copy-start.1
Sparse Core Ops, SparseCore 0:
  10.1 67.9 all-gather.4
  80.2 56.9 all-gather.6
  144.7 274.4 all-reduce.2
  508.0 127.0 all-reduce.4
where the time goes:
time: 644 us
  waiting for transfers between devices  532 us (83%)
  blocking collectives  73 us (11%)
  between operations  13.8 us (2%)
  other arithmetic  13.1 us (2%)
  matrix products  12.3 us (2%)
    psum x1, waiting for transfers between devices, body(): projected = lax.psum(p_local, ('col', 'rep')) / replicas  275 us
    psum x1, waiting for transfers between devices, body(): basis_next = lax.psum(right_local, ('row', 'rep')) / replicas  127 us
    psum x1, blocking collectives, body(): gram_matrix = lax.psum(gram_local, 'row')  73 us
    all_gather x1, waiting for transfers between devices, body(): whole_inputs = lax.all_gather(layer_inputs[0], 'col', axis=0, tiled=True)  69.3 us
    all_gather x1, waiting for transfers between devices, body(): whole_grads = lax.all_gather(output_grads[0], 'row', axis=0, tiled=True)  59.2 us
  transfers between devices with their start and end apart: 4, of which 4 were waited for; matrix products, arithmetic and copies ran while one was open for 0% of the time, Pallas kernels for 0%

commit v1 on v0

v1 whole, which is shorter than its diff:
```python
import jax
import jax.numpy as jnp
from jax import lax
from jax.experimental import pallas as pl
from jax.experimental.pallas import tpu as pltpu
from jax.sharding import PartitionSpec as P

MESH = pl.DeviceIdType.MESH
HIGH = lax.Precision.HIGHEST
F32 = jnp.float32
BF16 = jnp.bfloat16

RING = 16
HALF = 64
RANK = 64


def dot(a, b, dims, precision=None):
    return lax.dot_general(a, b, (dims, ((), ())), precision=precision, preferred_element_type=F32)


def kernel(
    x_ref, g_ref, e_ref, b_ref,
    comp_ref, ortho_ref, basis_ref,
    xg, gg, acc, sf_out, sf_in, sf_own, sf_all, s_mine, s_all, p_mine, p_peer,
    gram_mine, gram_all, mat, u_out, u_in, u_own, u_all,
    loc_sem, xr_send, xr_recv, xl_send, xl_recv, g_send, g_recv, d_send, d_recv,
    sf_send, sf_recv, sa_send, sa_recv, s_send, s_recv, p_send, p_recv,
    gr_send, gr_recv, u_send, u_recv, ua_send, ua_recv,
):
    row, col, rep = lax.axis_index("row"), lax.axis_index("col"), lax.axis_index("rep")
    y, x, core = row // 4, (row // 2) % 2, row % 2

    def at_row(yy, xx, cc):
        return lax.rem(yy + 4, 4) * 4 + xx * 2 + cc

    def wrap(v):
        return lax.rem(v + RING, RING)

    def remote(src, dst, ssem, rsem, where):
        return pltpu.make_async_remote_copy(
            src_ref=src, dst_ref=dst, send_sem=ssem, recv_sem=rsem,
            device_id=where, device_id_type=MESH,
        )

    here = (row, col, 1 - rep)
    sends = []

    def send(src, dst, ssem, rsem, where):
        copy = remote(src, dst, ssem, rsem, where)
        copy.start()
        sends.append(copy)

    def arrived(dst, rsem):
        remote(dst, dst, rsem, rsem, here).wait_recv()

    barrier = pltpu.get_barrier_semaphore()

    def signal(where):
        pl.semaphore_signal(barrier, inc=1, device_id=where, device_id_type=MESH)

    @pl.loop(1, RING)
    def _(k):
        signal((row, wrap(col + k), rep))
        signal((wrap(row + k), col, rep))
        signal((wrap(row + k), col, 1 - rep))

    signal((row, col, 1 - rep))

    own_x = pltpu.make_async_copy(x_ref.at[0], xg.at[col], loc_sem.at[0])
    own_g = pltpu.make_async_copy(g_ref.at[0], gg.at[row], loc_sem.at[1])
    own_x.start()
    own_g.start()
    own_x.wait()
    own_g.wait()

    b_t = b_ref[...].T
    st = dot(b_t, gg[row], ((1,), (1,))).astype(BF16)
    ft = dot(b_t, e_ref[0], ((1,), (1,))).astype(BF16)
    for a in range(4):
        rows = slice(16 * a, 16 * a + 16)
        sf_out[4 * a] = st[rows, :]
        for b in range(3):
            sf_out[4 * a + b + 1] = ft[rows, 128 * b:128 * b + 128]

    pl.semaphore_wait(barrier, 3 * (RING - 1) + 1)

    @pl.loop(1, RING)
    def _(k):
        to = wrap(col + k)
        remote(sf_out.at[to], sf_in.at[col], sf_send, sf_recv, (row, to, rep)).start()

    sf_in[col] = sf_out[col]

    right, left = (row, wrap(col + 1), rep), (row, wrap(col - 1), rep)
    send(xg.at[col], xg.at[col], xr_send.at[0], xr_recv.at[0], right)
    send(xg.at[col], xg.at[col], xl_send.at[0], xl_recv.at[0], left)

    up, down, side, sib = (
        (at_row(y + 1, x, core), col, rep),
        (at_row(y - 1, x, core), col, rep),
        (at_row(y, 1 - x, core), col, rep),
        (at_row(y, x, 1 - core), col, rep),
    )
    XP, YM, YP, YMX, YPX, Y2A, Y2B, X2A, X2B, OWN = range(10)
    place = {
        OWN: (0, 0, None), XP: (0, 1, None), YM: (-1, 0, None), YP: (1, 0, None),
        YMX: (-1, 1, None), YPX: (1, 1, None), Y2A: (2, 0, 0), Y2B: (2, 0, 1),
        X2A: (2, 1, 0), X2B: (2, 1, 1),
    }

    def block(name, cc):
        dy, dx, half = place[name]
        slot = at_row(y + dy, x if dx == 0 else 1 - x, cc)
        return gg.at[slot] if half is None else gg.at[slot, pl.ds(half * HALF, HALF)]

    def push(src, k, dst, where):
        ref = block(src, core)
        if dst in (Y2A, Y2B):
            dy, dx, _ = place[src]
            half = 0 if dst == Y2A else 1
            ref = gg.at[at_row(y + dy, x, core), pl.ds(half * HALF, HALF)]
        send(ref, ref, g_send.at[k], g_recv.at[dst], where)

    def got(name):
        arrived(block(name, core), g_recv.at[name])
        share(name)

    def share(name):
        ref = block(name, core)
        send(ref, ref, d_send.at[name], d_recv.at[name], sib)

    def shared(name):
        arrived(block(name, 1 - core), d_recv.at[name])

    push(OWN, 0, XP, side)
    push(OWN, 1, YM, up)
    push(OWN, 2, YP, down)
    share(OWN)

    def x_step(s):
        frm, tol = wrap(col - s), wrap(col + s)
        if s < 8:
            arrived(xg.at[frm], xr_recv.at[s - 1])
            ref = xg.at[frm] if s < 7 else xg.at[frm, pl.ds(0, HALF)]
            send(ref, ref, xr_send.at[s], xr_recv.at[s], right)
            arrived(xg.at[tol], xl_recv.at[s - 1])
            ref = xg.at[tol] if s < 7 else xg.at[tol, pl.ds(HALF, HALF)]
            send(ref, ref, xl_send.at[s], xl_recv.at[s], left)
        else:
            arrived(xg.at[frm, pl.ds(0, HALF)], xr_recv.at[7])
            arrived(xg.at[tol, pl.ds(HALF, HALF)], xl_recv.at[7])

    x_step(1)

    def many(ref, sem):
        remote(ref, ref, sem, sem, here).wait_recv()

    def many_sent(ref, sem):
        remote(ref, ref, sem, sem, here).wait_send()

    many(sf_in.at[pl.ds(0, RING - 1)], sf_recv)
    sf_own[...] = jnp.sum(sf_in[...].astype(F32), axis=0).astype(BF16)

    @pl.loop(1, RING)
    def _(k):
        to = wrap(col + k)
        remote(sf_own, sf_all.at[col], sa_send, sa_recv, (row, to, rep)).start()

    sf_all[col] = sf_own[...]
    x_step(2)
    many(sf_all.at[pl.ds(0, RING - 1)], sa_recv)
    for a in range(4):
        s_mine[16 * a:16 * a + 16, :] = sf_all[4 * a]

    @pl.loop(1, RING)
    def _(k):
        to = wrap(row + k)
        remote(s_mine, s_all.at[row], s_send, s_recv, (to, col, rep)).start()

    s_all[row] = s_mine[...]
    x_step(3)
    got(YM)
    push(YM, 3, Y2A, up)
    got(YP)
    push(YP, 4, Y2B, down)
    got(XP)
    push(XP, 5, YMX, up)
    push(XP, 6, YPX, down)
    x_step(4)
    x_step(5)
    x_step(6)
    x_step(7)
    got(Y2A)
    push(Y2A, 7, X2A, side)
    got(Y2B)
    push(Y2B, 8, X2B, side)
    many(s_all.at[pl.ds(0, RING - 1)], s_recv)
    x_step(8)

    s_wide = jnp.concatenate([s_all[t] for t in range(RING)], axis=1)
    f_wide = jnp.concatenate(
        [jnp.concatenate([sf_all[4 * a + b + 1] for a in range(4)], axis=0) for b in range(3)],
        axis=1,
    )
    p_part = dot(s_wide, xg[...].reshape(RING * 128, 384), ((1,), (0,)))
    p_mine[...] = (p_part + f_wide.astype(F32)).astype(BF16)
    send(p_mine, p_peer, p_send, p_recv, (row, col, 1 - rep))

    def multiply(first, yy, xx):
        pair = lax.rem(yy + 4, 4) * 2 + xx
        xs = xg[pl.ds(2 * pair, 2)].reshape(256, 384)

        @pl.loop(0, 3)
        def _(n):
            cols = pl.ds(pl.multiple_of(n * 512, 512), 512)
            gs = gg[pl.ds(2 * pair, 2), :, cols].reshape(256, 512)
            if first:
                acc[:, cols] = e_ref[0, :, cols].astype(F32) + dot(xs, gs, ((0,), (0,)))
            else:
                acc[:, cols] += dot(xs, gs, ((0,), (0,)))

    shared(OWN)
    multiply(True, y, x)

    arrived(p_peer, p_recv)
    p_t = (p_mine[...].astype(F32) + p_peer[...].astype(F32)) * 0.5
    gram = dot(p_t, p_t, ((1,), (1,)), HIGH)
    gram_mine[...] = jnp.concatenate([gram[:32], gram[32:]], axis=1)

    @pl.loop(1, RING)
    def _(k):
        to = wrap(row + k)
        remote(gram_mine, gram_all.at[row], gr_send, gr_recv, (to, col, rep)).start()

    gram_all[row] = gram_mine[...]

    shared(XP)
    multiply(False, y, 1 - x)
    shared(YM)
    multiply(False, y - 1, x)
    shared(YP)
    multiply(False, y + 1, x)

    many(gram_all.at[pl.ds(0, RING - 1)], gr_recv)
    total = jnp.sum(gram_all[...], axis=0)
    gram = jnp.concatenate([total[:, :RANK], total[:, RANK:]], axis=0)
    subl = lax.broadcasted_iota(jnp.int32, (RANK, 128), 0)
    lane = lax.broadcasted_iota(jnp.int32, (RANK, 128), 1)
    mat[...] = jnp.concatenate([gram, (subl == lane)[:, :RANK].astype(F32)], axis=1)

    def eliminate(k, carry):
        m = mat[...]
        pivot_row = mat[pl.ds(k, 1), :]
        column = jnp.sum(jnp.where(lane == k, m, 0.0), axis=1, keepdims=True)
        pivot = jnp.sum(jnp.where(lane[:1] == k, pivot_row, 0.0), axis=1, keepdims=True)
        factor = jnp.where(subl[:, :1] > k, column / pivot, 0.0)
        mat[...] = m - factor * pivot_row
        return carry

    lax.fori_loop(0, RANK, eliminate, 0)

    got(YMX)
    got(YPX)
    shared(Y2A)
    shared(Y2B)
    multiply(False, y + 2, x)
    shared(YMX)
    multiply(False, y - 1, 1 - x)
    shared(YPX)
    multiply(False, y + 1, 1 - x)
    got(X2A)
    got(X2B)
    shared(X2A)
    shared(X2B)
    multiply(False, y + 2, 1 - x)

    comp_ref[...] = acc[...].astype(BF16)

    p_low = p_t.astype(BF16)
    for b in range(4):
        cols = slice(384 * b, 384 * b + 384)
        ut = dot(p_low, comp_ref[:, cols], ((1,), (0,))).astype(BF16)
        for a in range(4):
            u_out[4 * a + b] = ut[16 * a:16 * a + 16, :]

    me = row + RING * rep
    mine = row // 2 + 8 * rep
    owner = core == x

    def piece_at(k):
        chip = lax.rem(k, 8)
        return (2 * chip + lax.rem(chip, 2), col, k // 8)

    @pl.loop(0, RING)
    def _(k):
        @pl.when(jnp.logical_not(jnp.logical_and(owner, k == mine)))
        def _():
            remote(u_out.at[k], u_in.at[me], u_send, u_recv, piece_at(k)).start()

    d = jnp.sum(jnp.where(lane == subl, mat[...], 0.0), axis=1, keepdims=True)
    inv_factor = lax.rsqrt(d) * mat[:, RANK:]

    ortho_ref[...] = dot(inv_factor, p_t, ((1,), (0,)), HIGH).astype(BF16)

    @pl.when(owner)
    def _():
        u_in[me] = u_out[mine]
        many(u_in.at[pl.ds(0, 31)], u_recv)
        u_own[...] = jnp.sum(u_in[...].astype(F32), axis=0).astype(BF16)

        @pl.loop(1, 32)
        def _(k):
            to = lax.rem(me + k, 32)
            remote(u_own, u_all.at[mine], ua_send, ua_recv, (lax.rem(to, RING), col, to // RING)).start()

        u_all[mine] = u_own[...]
        many(u_all.at[pl.ds(0, 15)], ua_recv)
        many_sent(u_out.at[pl.ds(0, 15)], u_send)
        many_sent(u_in.at[pl.ds(0, 31)], ua_send)

    @pl.when(jnp.logical_not(owner))
    def _():
        many(u_all, ua_recv)
        many_sent(u_out, u_send)

    for b in range(4):
        ut = jnp.concatenate([u_all[4 * a + b] for a in range(4)], axis=0).astype(F32) * 0.5
        basis_ref[:, 384 * b:384 * b + 384] = dot(inv_factor, ut, ((1,), (0,)), HIGH)

    for copy in sends:
        copy.wait_send()
    many_sent(sf_out.at[pl.ds(0, 15)], sf_send)
    many_sent(sf_in.at[pl.ds(0, 15)], sa_send)
    many_sent(s_all.at[pl.ds(0, 15)], s_send)
    many_sent(gram_all.at[pl.ds(0, 15)], gr_send)


def body(layer_inputs, output_grads, error_prev, basis_prev):
    dma = pltpu.SemaphoreType.DMA
    comp, ortho_t, basis_t = pl.pallas_call(
        kernel,
        out_shape=(
            jax.ShapeDtypeStruct((384, 1536), BF16),
            jax.ShapeDtypeStruct((RANK, 384), BF16),
            jax.ShapeDtypeStruct((RANK, 1536), F32),
        ),
        in_specs=[
            pl.BlockSpec(memory_space=pl.ANY),
            pl.BlockSpec(memory_space=pl.ANY),
            pl.BlockSpec(memory_space=pltpu.VMEM),
            pl.BlockSpec(memory_space=pltpu.VMEM),
        ],
        out_specs=[pl.BlockSpec(memory_space=pltpu.VMEM)] * 3,
        scratch_shapes=[
            pltpu.VMEM((16, 128, 384), BF16),
            pltpu.VMEM((16, 128, 1536), BF16),
            pltpu.VMEM((384, 1536), F32),
            pltpu.VMEM((16, 16, 128), BF16),
            pltpu.VMEM((16, 16, 128), BF16),
            pltpu.VMEM((16, 128), BF16),
            pltpu.VMEM((16, 16, 128), BF16),
            pltpu.VMEM((64, 128), BF16),
            pltpu.VMEM((16, 64, 128), BF16),
            pltpu.VMEM((64, 384), BF16),
            pltpu.VMEM((64, 384), BF16),
            pltpu.VMEM((32, 128), F32),
            pltpu.VMEM((16, 32, 128), F32),
            pltpu.VMEM((64, 128), F32),
            pltpu.VMEM((16, 16, 384), BF16),
            pltpu.VMEM((32, 16, 384), BF16),
            pltpu.VMEM((16, 384), BF16),
            pltpu.VMEM((16, 16, 384), BF16),
            dma((2,)),
            dma((8,)), dma((8,)), dma((8,)), dma((8,)),
            dma((9,)), dma((9,)), dma((10,)), dma((10,)),
        ] + [dma(())] * 14,
        compiler_params=pltpu.CompilerParams(
            collective_id=0, has_side_effects=True, vmem_limit_bytes=48 * 2**20
        ),
        name="powersgd",
    )(layer_inputs, output_grads, error_prev, basis_prev)
    basis_next = basis_t.T
    approx = dot(ortho_t, basis_t.astype(BF16), ((0,), (0,)))
    error_next = (comp.astype(F32) - approx).astype(BF16)
    return (basis_next, error_next[None])


def solution(mesh):
    return jax.shard_map(
        body,
        mesh=mesh,
        in_specs=(
            P("rep", "col", "row"),
            P("rep", "row", "col"),
            P("rep", "row", "col"),
            P("col", None),
        ),
        out_specs=(P("col", None), P("rep", "row", "col")),
        check_vma=False,
    )
```

time: 644 us -> 97.6 us (0.15)
  waiting for transfers between devices: 532 us -> 0 us
  Pallas kernels: 0 us -> 90.1 us
  blocking collectives: 73 us -> 0 us
  between operations: 13.8 us -> 0.66 us
  other arithmetic: 13.1 us -> 0 us
  matrix products: 12.3 us -> 1.51 us
    psum x2 -> x0, waiting for transfers between devices: 402 us -> none  [the longest x1 275 us: body(): projected = lax.psum(p_local, ('col', 'rep')) / replicas]
    all_gather x2 -> x0, waiting for transfers between devices: 129 us -> none  [the longest x1 69.3 us: body(): whole_inputs = lax.all_gather(layer_inputs[0], 'col', axis=0, tiled=True)]
    pallas_call x0 -> x1, Pallas kernels: none -> 90.1 us  [body(): pl.pallas_call(kernel, out_shape=(jax.ShapeDtypeStruct((384, 1536), BF16)...]
    psum x1 -> x0, blocking collectives: 73 us -> none  [body(): gram_matrix = lax.psum(gram_local, 'row')]
    another operation x5 -> x0, other arithmetic: 12.1 us -> none  [the longest x3 6.52 us: body(): factor = jnp.linalg.cholesky(gram_matrix)]
    dot_general x5 -> x1, matrix products: 11.1 us -> 1.51 us  [dot(): lax.dot_general(a, b, (dims, ((), ())), precision=precision, preferred_el...]
  transfers between devices with their start and end apart: 4 -> 0, of which waited for: 4 -> 0; matrix products, arithmetic and copies ran while one was open for 0% -> 0% of each run, Pallas kernels for 0% -> 0%
where the time goes in v1:
time: 97.6 us; the launch traced here: 97.3 us
  Pallas kernels  90.1 us (92%)
  local copies, waits for them, and re-layouts  5.05 us (5%)
  matrix products  1.51 us (2%)
    pallas_call x1, Pallas kernels, body(): pl.pallas_call(kernel, out_shape=(jax.ShapeDtypeStruct((384, 1536), BF16)...  90.1 us
    unnamed x8, local copies, waits for them, and re-layouts  5.05 us

profile of v1, /device:TPU:1, one launch (start us, length us, event | category | flops | bytes accessed | tf_op | source)
XLA Modules:
  0.0 97.3 jit_solution(16695438460419174799)
XLA Ops:
  0.6 1.1 %copy.6.b_ref = bf16[1536,64]{1,0:T(8,128)(2,1)S(1)} copy(bf16[1536,64]{0,1:T(8,128)(2,1)} %param.7) | data formatting | bytes 393216 | tf_op args[3]
  1.8 0.0 copy-start
  1.8 1.3 %copy-done = bf16[1,384,1536]{2,1,0:T(8,128)(2,1)S(1)} copy-done((bf16[1,384,1536]{2,1,0:T(8,128)(2,1)S(1)}, bf16[1,384,1536]{2,1,0:T(8,128)(2,1)}, u32[]{:S(2)}) %copy-start) | copy-done | bytes 1179672
  3.1 0.0 copy-start.1
  3.1 1.0 %copy-done.1 = bf16[1,128,1536]{2,1,0:T(8,128)(2,1)S(1)} copy-done((bf16[1,128,1536]{2,1,0:T(8,128)(2,1)S(1)}, bf16[1,128,1536]{2,1,0:T(8,128)(2,1)}, u32[]{:S(2)}) %copy-start.1) | copy-done | bytes 393240
  4.1 0.0 copy-start.2
  4.1 0.9 copy-done.2
  4.9 90.1 %powersgd.1 = (bf16[384,1536]{1,0:T(8,128)(2,1)S(1)}, bf16[64,384]{1,0:T(8,128)(2,1)S(1)}, f32[64,1536]{1,0:T(8,128)S(1)}) custom-call(bf16[1,128,384]{2,1,0:T(8,128)(2,1)S(1)} %copy-done.2, bf16[1,128,1536]{2,1,0:T(8,128)(2,1)S(1)} %copy-done.1, bf16[1,384,1536]{2,1,0:T(8,128)(2,1)S(1)} %copy-done, bf16[1536,64]{1,0:T(8,128)(2,1)S(1)} %copy.6.b_ref), custom_call_target="tpu_custom_call" | custom-call | tf_op jit(solution)/shard_map/powersgd/pallas_call | solution.py:341
  95.1 1.5 %fusion.1 = bf16[1,384,1536]{2,1,0:T(8,128)(2,1)} fusion(bf16[64,384]{1,0:T(8,128)(2,1)S(1)} %get-tuple-element.7, bf16[384,1536]{1,0:T(8,128)(2,1)S(1)} %get-tuple-element.6, f32[64,1536]{1,0:T(8,128)S(1)} %get-tuple-element.5), kind=kOutput, calls=%fused_computation.2 | convolution fusion | flops 77365248 | bytes 2801664 | tf_op jit(solution)/shard_map/dot_general | solution.py:19
  96.6 0.7 copy.8
Async XLA Ops:
  1.8 1.3 %copy-start = (bf16[1,384,1536]{2,1,0:T(8,128)(2,1)S(1)}, bf16[1,384,1536]{2,1,0:T(8,128)(2,1)}, u32[]{:S(2)}) copy-start(bf16[1,384,1536]{2,1,0:T(8,128)(2,1)} %e_ref.1) | copy-start | bytes 3538948
  3.1 1.0 %copy-start.1 = (bf16[1,128,1536]{2,1,0:T(8,128)(2,1)S(1)}, bf16[1,128,1536]{2,1,0:T(8,128)(2,1)}, u32[]{:S(2)}) copy-start(bf16[1,128,1536]{2,1,0:T(8,128)(2,1)} %g_ref.1) | copy-start | bytes 1179652
  4.1 0.9 copy-start.2

commit v2 on v1

v2 whole, which is shorter than its diff:
```python
import jax
import jax.numpy as jnp
from jax import lax
from jax.experimental import pallas as pl
from jax.experimental.pallas import tpu as pltpu
from jax.sharding import PartitionSpec as P

MESH = pl.DeviceIdType.MESH
HIGH = lax.Precision.HIGHEST
F32 = jnp.float32
BF16 = jnp.bfloat16

RING = 16
HALF = 64
RANK = 64


def dot(a, b, dims, precision=None):
    return lax.dot_general(a, b, (dims, ((), ())), precision=precision, preferred_element_type=F32)


def kernel(
    x_ref, g_ref, e_ref, bt_ref,
    comp_ref, ortho_ref, basis_ref,
    xg, gg, acc, xt, e_in, bt, s_one, s_two, f_out, f_in, f_own, f_all, s_all, p_mine, p_peer,
    gram_mine, gram_all, mat, u_out, u_in, u_own, u_all,
    loc_sem, x_send, xr_recv, xl_recv, g_send, g_recv, d_send, d_recv,
    s_send, s_recv, f_send, f_recv, r_send, r_recv, p_send, p_recv, gr_send, gr_recv, u_send, u_recv, near,
):
    row, col, rep = lax.axis_index("row"), lax.axis_index("col"), lax.axis_index("rep")
    y, x, core = row // 4, (row // 2) % 2, row % 2

    def at_row(yy, xx, cc):
        return lax.rem(yy + 4, 4) * 4 + xx * 2 + cc

    def wrap(v):
        return lax.rem(v + RING, RING)

    def remote(src, dst, ssem, rsem, where):
        return pltpu.make_async_remote_copy(
            src_ref=src, dst_ref=dst, send_sem=ssem, recv_sem=rsem,
            device_id=where, device_id_type=MESH,
        )

    here = (row, col, 1 - rep)
    sends = []

    def send(src, dst, ssem, rsem, where):
        copy = remote(src, dst, ssem, rsem, where)
        copy.start()
        sends.append(copy)

    def arrived(dst, rsem):
        remote(dst, dst, rsem, rsem, here).wait_recv()

    def sent(src, ssem):
        remote(src, src, ssem, ssem, here).wait_send()

    own_g = pltpu.make_async_copy(g_ref.at[0], gg.at[row], loc_sem.at[0])
    own_b = pltpu.make_async_copy(bt_ref, bt, loc_sem.at[1])
    own_x = pltpu.make_async_copy(x_ref.at[0], xg.at[col], loc_sem.at[2])
    own_e = pltpu.make_async_copy(e_ref.at[0], e_in, loc_sem.at[3])
    for copy in (own_g, own_b, own_x, own_e):
        copy.start()

    barrier = pltpu.get_barrier_semaphore()

    def signal(where):
        pl.semaphore_signal(barrier, inc=1, device_id=where, device_id_type=MESH)

    right, left = (row, wrap(col + 1), rep), (row, wrap(col - 1), rep)
    up, down, side, sib = (
        (at_row(y + 1, x, core), col, rep),
        (at_row(y - 1, x, core), col, rep),
        (at_row(y, 1 - x, core), col, rep),
        (at_row(y, x, 1 - core), col, rep),
    )
    for where in (right, left, up, down, side, sib, here):
        signal(where)

    def tell(k, *to):
        for where in to:
            pl.semaphore_signal(near.at[k], inc=1, device_id=where, device_id_type=MESH)

    def told(k, count):
        pl.semaphore_wait(near.at[k], count)

    own_g.wait()
    own_b.wait()
    quarter, group = lax.rem(col, 4), col // 4
    s_one[quarter] = dot(bt[...], gg[row], ((1,), (1,))).astype(BF16)
    own_x.wait()

    pl.semaphore_wait(barrier, 7)
    plane = (up, down, side, sib)

    def x_half(owner, half):
        return xg.at[owner, pl.ds(half * HALF, HALF)]

    def x_push(owner, half, k, side):
        ref = x_half(owner, half)
        recv = (xr_recv if side == 0 else xl_recv).at[2 * k + half]
        send(ref, ref, x_send.at[side, 2 * k + half], recv, right if side == 0 else left)

    for half in range(2):
        x_push(col, half, 0, 0)
        x_push(col, 1 - half, 0, 1)

    def x_step(k):
        frm, to = wrap(col - k), wrap(col + k)
        for i in range(2):
            half = i
            if k < 8 or half == 0:
                arrived(x_half(frm, half), xr_recv.at[2 * k - 2 + half])
                if k < 7 or (k == 7 and half == 0):
                    x_push(frm, half, k, 0)
            half = 1 - i
            if k < 8 or half == 1:
                arrived(x_half(to, half), xl_recv.at[2 * k - 2 + half])
                if k < 7 or (k == 7 and half == 1):
                    x_push(to, half, k, 1)

    XP, YM, YP, YMX, YPX, Y2A, Y2B, X2A, X2B, OWN = range(10)
    place = {
        OWN: (0, 0, None), XP: (0, 1, None), YM: (-1, 0, None), YP: (1, 0, None),
        YMX: (-1, 1, None), YPX: (1, 1, None), Y2A: (2, 0, 0), Y2B: (2, 0, 1),
        X2A: (2, 1, 0), X2B: (2, 1, 1),
    }

    def block(name, cc):
        dy, dx, half = place[name]
        slot = at_row(y + dy, x if dx == 0 else 1 - x, cc)
        return gg.at[slot] if half is None else gg.at[slot, pl.ds(half * HALF, HALF)]

    def push(src, k, dst, where):
        ref = block(src, core)
        if dst in (Y2A, Y2B):
            dy, dx, _ = place[src]
            half = 0 if dst == Y2A else 1
            ref = gg.at[at_row(y + dy, x, core), pl.ds(half * HALF, HALF)]
        send(ref, ref, g_send.at[k], g_recv.at[dst], where)

    def got(name):
        arrived(block(name, core), g_recv.at[name])
        share(name)

    def share(name):
        ref = block(name, core)
        send(ref, ref, d_send.at[name], d_recv.at[name], sib)

    def shared(name):
        arrived(block(name, 1 - core), d_recv.at[name])

    push(OWN, 0, XP, side)
    push(OWN, 1, YM, up)
    push(OWN, 2, YP, down)
    share(OWN)
    tell(0, right, left)
    tell(3, *plane)

    own_e.wait()
    ft = dot(bt[...], e_in[...], ((1,), (1,))).astype(BF16)
    for a in range(4):
        for b in range(3):
            f_out[4 * a + b + 1] = ft[16 * a:16 * a + 16, 128 * b:128 * b + 128]
    f_owner = quarter > 0
    f_count = 12

    told(0, 2)
    tell(1, (row, wrap(col + 2), rep), (row, wrap(col - 2), rep))
    told(3, 4)
    tell(4, *plane)
    told(1, 2)
    tell(2, (row, wrap(col + 4), rep), (row, wrap(col - 4), rep))

    for k in range(1, 4):
        to = lax.rem(quarter + k, 4)
        send(s_one.at[quarter], s_one.at[quarter], s_send.at[0, k], s_recv.at[0, k], (row, group * 4 + to, rep))

    x_step(1)
    told(4, 4)
    tell(5, *plane)
    told(2, 2)

    @pl.loop(1, RING)
    def _(k):
        to = wrap(col + k)

        @pl.when(lax.rem(to, 4) > 0)
        def _():
            remote(f_out.at[to], f_in.at[col], f_send.at[0], f_recv.at[0], (row, to, rep)).start()

    x_step(2)
    for k in range(1, 4):
        arrived(s_one.at[lax.rem(quarter + 4 - k, 4)], s_recv.at[0, k])
    s_two[group] = jnp.sum(s_one[...].astype(F32), axis=0).astype(BF16)
    for k in range(1, 4):
        to = lax.rem(group + k, 4)
        send(s_two.at[group], s_two.at[group], s_send.at[1, k], s_recv.at[1, k], (row, to * 4 + quarter, rep))
    told(5, 4)
    tell(6, here)
    x_step(3)
    got(YM)
    push(YM, 3, Y2A, up)
    got(YP)
    push(YP, 4, Y2B, down)
    got(XP)
    push(XP, 5, YMX, up)
    push(XP, 6, YPX, down)
    x_step(4)

    @pl.when(f_owner)
    def _():
        f_in[col] = f_out[col]
        arrived(f_in.at[pl.ds(0, RING - 1)], f_recv.at[0])
        f_own[...] = jnp.sum(f_in[...].astype(F32), axis=0).astype(BF16)

        @pl.loop(1, RING)
        def _(k):
            remote(f_own, f_all.at[col], f_send.at[1], f_recv.at[1], (row, wrap(col + k), rep)).start()

        f_all[col] = f_own[...]
        sent(f_out.at[pl.ds(0, f_count - 1)], f_send.at[0])
        sent(f_in.at[pl.ds(0, RING - 1)], f_send.at[1])

    for k in range(1, 4):
        arrived(s_two.at[lax.rem(group + 4 - k, 4)], s_recv.at[1, k])
    s_all[row] = jnp.sum(s_two[...].astype(F32), axis=0).astype(BF16)

    @pl.loop(1, RING)
    def _(k):
        remote(s_all.at[row], s_all.at[row], r_send.at[0], r_recv.at[0], (wrap(row + k), col, rep)).start()

    x_step(5)
    got(Y2A)
    push(Y2A, 7, X2A, side)
    got(Y2B)
    push(Y2B, 8, X2B, side)
    x_step(6)

    @pl.when(f_owner)
    def _():
        arrived(f_all.at[pl.ds(0, f_count - 1)], f_recv.at[1])

    @pl.when(jnp.logical_not(f_owner))
    def _():
        arrived(f_all.at[pl.ds(0, f_count)], f_recv.at[1])
        sent(f_out.at[pl.ds(0, f_count)], f_send.at[0])

    x_step(7)
    arrived(s_all.at[pl.ds(0, RING - 1)], r_recv.at[0])
    x_step(8)

    s_wide = jnp.concatenate([s_all[t] for t in range(RING)], axis=1)
    f_wide = jnp.concatenate(
        [jnp.concatenate([f_all[4 * a + b + 1] for a in range(4)], axis=0) for b in range(3)],
        axis=1,
    )
    p_part = dot(s_wide, xg[...].reshape(RING * 128, 384), ((1,), (0,)))
    p_mine[...] = p_part + f_wide.astype(F32)
    send(p_mine, p_peer, p_send, p_recv, (row, col, 1 - rep))

    def multiply(first, yy, xx):
        pair = lax.rem(yy + 4, 4) * 2 + xx
        xt[...] = xg[pl.ds(2 * pair, 2)].reshape(256, 384).T

        @pl.loop(0, 3)
        def _(n):
            cols = pl.ds(pl.multiple_of(n * 512, 512), 512)
            gs = gg[pl.ds(2 * pair, 2), :, cols].reshape(256, 512)
            if first:
                acc[:, cols] = e_in[:, cols].astype(F32) + dot(xt[...], gs, ((1,), (0,)))
            else:
                acc[:, cols] += dot(xt[...], gs, ((1,), (0,)))

    shared(OWN)
    multiply(True, y, x)
    shared(XP)
    multiply(False, y, 1 - x)
    shared(YM)
    multiply(False, y - 1, x)
    shared(YP)
    multiply(False, y + 1, x)
    got(YMX)
    got(YPX)
    shared(Y2A)
    shared(Y2B)
    multiply(False, y + 2, x)
    shared(YMX)
    multiply(False, y - 1, 1 - x)
    shared(YPX)
    multiply(False, y + 1, 1 - x)
    got(X2A)
    got(X2B)
    shared(X2A)
    shared(X2B)
    multiply(False, y + 2, 1 - x)
    comp_ref[...] = acc[...].astype(BF16)

    told(6, 1)
    arrived(p_peer, p_recv)
    p_t = (p_mine[...] + p_peer[...]) * 0.5

    p_high = p_t.astype(BF16)
    p_rest = (p_t - p_high.astype(F32)).astype(BF16)
    p_both = jnp.concatenate([p_high, p_rest], axis=0)
    me = row + RING * rep
    mine = row // 2 + 8 * rep
    owner = core == x

    def piece_at(k):
        chip = lax.rem(k, 8)
        return (2 * chip + lax.rem(chip, 2), col, k // 8)

    for b in range(4):
        cols = slice(384 * b, 384 * b + 384)
        ut = dot(p_both, comp_ref[:, cols], ((1,), (0,)))
        ut = (ut[:RANK] + ut[RANK:]).astype(BF16)
        for a in range(4):
            u_out[4 * a + b] = ut[16 * a:16 * a + 16, :]

    @pl.loop(0, RING)
    def _(k):
        @pl.when(jnp.logical_not(jnp.logical_and(owner, k == mine)))
        def _():
            remote(u_out.at[k], u_in.at[me], u_send.at[0], u_recv.at[0], piece_at(k)).start()

    gram = dot(p_t, p_t, ((1,), (1,)), HIGH)
    gram_mine[...] = jnp.concatenate([gram[:32], gram[32:]], axis=1)

    @pl.loop(1, RING)
    def _(k):
        to = wrap(row + k)
        remote(gram_mine, gram_all.at[row], gr_send, gr_recv, (to, col, rep)).start()

    gram_all[row] = gram_mine[...]

    @pl.when(owner)
    def _():
        u_in[me] = u_out[mine]
        arrived(u_in.at[pl.ds(0, 31)], u_recv.at[0])
        u_own[...] = jnp.sum(u_in[...].astype(F32), axis=0).astype(BF16)

        @pl.loop(1, 32)
        def _(k):
            to = lax.rem(me + k, 32)
            remote(u_own, u_all.at[mine], u_send.at[1], u_recv.at[1], (lax.rem(to, RING), col, to // RING)).start()

        u_all[mine] = u_own[...]

    arrived(gram_all.at[pl.ds(0, RING - 1)], gr_recv)
    total = jnp.sum(gram_all[...], axis=0)
    gram = jnp.concatenate([total[:, :RANK], total[:, RANK:]], axis=0)
    subl = lax.broadcasted_iota(jnp.int32, (RANK, 128), 0)
    lane = lax.broadcasted_iota(jnp.int32, (RANK, 128), 1)
    mat[...] = jnp.concatenate([gram, (subl == lane)[:, :RANK].astype(F32)], axis=1)

    def eliminate(k, carry):
        m = mat[...]
        pivot_row = mat[pl.ds(k, 1), :]
        column = jnp.sum(jnp.where(lane == k, m, 0.0), axis=1, keepdims=True)
        pivot = jnp.sum(jnp.where(lane[:1] == k, pivot_row, 0.0), axis=1, keepdims=True)
        factor = jnp.where(subl[:, :1] > k, column / pivot, 0.0)
        mat[...] = m - factor * pivot_row
        return carry

    lax.fori_loop(0, RANK, eliminate, 0)
    d = jnp.sum(jnp.where(lane == subl, mat[...], 0.0), axis=1, keepdims=True)
    inv_factor = lax.rsqrt(d) * mat[:, RANK:]
    ortho_ref[...] = dot(inv_factor, p_t, ((1,), (0,)), HIGH).astype(BF16)

    @pl.when(owner)
    def _():
        arrived(u_all.at[pl.ds(0, 15)], u_recv.at[1])
        sent(u_out.at[pl.ds(0, 15)], u_send.at[0])
        sent(u_in.at[pl.ds(0, 31)], u_send.at[1])

    @pl.when(jnp.logical_not(owner))
    def _():
        arrived(u_all, u_recv.at[1])
        sent(u_out, u_send.at[0])

    for b in range(4):
        ut = jnp.concatenate([u_all[4 * a + b] for a in range(4)], axis=0).astype(F32) * 0.5
        basis_ref[:, 384 * b:384 * b + 384] = dot(inv_factor, ut, ((1,), (0,)), HIGH)

    for copy in sends:
        copy.wait_send()
    sent(s_all.at[pl.ds(0, 15)], r_send.at[0])
    sent(gram_all.at[pl.ds(0, 15)], gr_send)


def body(layer_inputs, output_grads, error_prev, basis_prev):
    dma = pltpu.SemaphoreType.DMA
    vmem = pltpu.VMEM
    comp, ortho_t, basis_t = pl.pallas_call(
        kernel,
        out_shape=(
            jax.ShapeDtypeStruct((384, 1536), BF16),
            jax.ShapeDtypeStruct((RANK, 384), BF16),
            jax.ShapeDtypeStruct((RANK, 1536), F32),
        ),
        in_specs=[pl.BlockSpec(memory_space=pl.ANY)] * 4,
        out_specs=[pl.BlockSpec(memory_space=vmem)] * 3,
        scratch_shapes=[
            vmem((16, 128, 384), BF16),
            vmem((16, 128, 1536), BF16),
            vmem((384, 1536), F32),
            vmem((384, 256), BF16),
            vmem((384, 1536), BF16),
            vmem((RANK, 1536), BF16),
            vmem((4, RANK, 128), BF16),
            vmem((4, RANK, 128), BF16),
            vmem((16, 16, 128), BF16),
            vmem((16, 16, 128), BF16),
            vmem((16, 128), BF16),
            vmem((16, 16, 128), BF16),
            vmem((16, RANK, 128), BF16),
            vmem((RANK, 384), F32),
            vmem((RANK, 384), F32),
            vmem((32, 128), F32),
            vmem((16, 32, 128), F32),
            vmem((RANK, 128), F32),
            vmem((16, 16, 384), BF16),
            vmem((32, 16, 384), BF16),
            vmem((16, 384), BF16),
            vmem((16, 16, 384), BF16),
            dma((4,)),
            dma((2, 16)), dma((16,)), dma((16,)),
            dma((9,)), dma((9,)), dma((10,)), dma((10,)),
            dma((2, 4)), dma((2, 4)), dma((2,)), dma((2,)), dma((1,)), dma((1,)),
            dma(()), dma(()), dma(()), dma(()), dma((2,)), dma((2,)),
            pltpu.SemaphoreType.REGULAR((7,)),
        ],
        compiler_params=pltpu.CompilerParams(
            collective_id=0, has_side_effects=True, vmem_limit_bytes=60 * 2**20
        ),
        name="powersgd",
    )(layer_inputs, output_grads, error_prev, basis_prev.T)
    basis_next = basis_t.T
    approx = dot(ortho_t, basis_t.astype(BF16), ((0,), (0,)))
    error_next = (comp.astype(F32) - approx).astype(BF16)
    return (basis_next, error_next[None])


def solution(mesh):
    return jax.shard_map(
        body,
        mesh=mesh,
        in_specs=(
            P("rep", "col", "row"),
            P("rep", "row", "col"),
            P("rep", "row", "col"),
            P("col", None),
        ),
        out_specs=(P("col", None), P("rep", "row", "col")),
        check_vma=False,
    )
```

time: 97.6 us -> 78.3 us (0.80)
  Pallas kernels: 90.1 us -> 73.8 us
  local copies, waits for them, and re-layouts: 5.05 us -> 0.75 us
  matrix products: 1.51 us -> 2.97 us
    pallas_call x1, Pallas kernels: 90.1 us -> 73.8 us  [body(): pl.pallas_call(kernel, out_shape=(jax.ShapeDtypeStruct((384, 1536), BF16)...]
    unnamed x8 -> x3, local copies, waits for them, and re-layouts: 5.05 us -> 0.75 us
    dot_general x1, matrix products: 1.51 us -> 2.97 us  [dot(): lax.dot_general(a, b, (dims, ((), ())), precision=precision, preferred_el...]
where the time goes in v2:
time: 78.3 us; the launch traced here: 78.1 us
  Pallas kernels  73.8 us (94%)
  matrix products  2.97 us (4%)
    pallas_call x1, Pallas kernels, body(): pl.pallas_call(kernel, out_shape=(jax.ShapeDtypeStruct((384, 1536), BF16)...  73.8 us
    dot_general x1, matrix products, dot(): lax.dot_general(a, b, (dims, ((), ())), precision=precision, preferred_el...  2.97 us

profile of v2, /device:TPU:1, one launch (start us, length us, event | category | flops | bytes accessed | tf_op | source)
XLA Modules:
  0.0 78.1 jit_solution(17711674937977609145)
XLA Ops:
  0.6 73.8 %powersgd.1 = (bf16[384,1536]{1,0:T(8,128)(2,1)}, bf16[64,384]{1,0:T(8,128)(2,1)}, f32[64,1536]{1,0:T(8,128)}) custom-call(bf16[1,128,384]{2,1,0:T(8,128)(2,1)} %x_ref.1, bf16[1,128,1536]{2,1,0:T(8,128)(2,1)} %g_ref.1, bf16[1,384,1536]{2,1,0:T(8,128)(2,1)} %e_ref.1, bf16[64,1536]{1,0:T(8,128)(2,1)} %bitcast.6), custom_call_target="tpu_custom_call" | custom-call | tf_op jit(solution)/shard_map/powersgd/pallas_call | solution.py:396
  74.4 0.0 copy-start
  74.4 3.0 %fusion.1 = bf16[1,384,1536]{2,1,0:T(8,128)(2,1)} fusion(bf16[64,384]{1,0:T(8,128)(2,1)} %get-tuple-element.7, bf16[384,1536]{1,0:T(8,128)(2,1)} %get-tuple-element.6, f32[64,1536]{1,0:T(8,128)} %get-tuple-element.5), kind=kOutput, calls=%fused_computation.2 | convolution fusion | flops 77365248 | bytes 2801664 | tf_op jit(solution)/shard_map/dot_general | solution.py:19
  77.4 0.0 copy-done
  77.4 0.7 copy.7
Async XLA Ops:
  74.4 3.0 %copy-start = (f32[64,1536]{1,0:T(8,128)S(1)}, f32[64,1536]{1,0:T(8,128)}, u32[]{:S(2)}) copy-start(f32[64,1536]{1,0:T(8,128)} %get-tuple-element.5) | copy-start | bytes 1179652

commit v3 on v2

v3 whole, which is shorter than its diff:
```python
import functools

import jax
import jax.numpy as jnp
from jax import lax
from jax.experimental import pallas as pl
from jax.experimental.pallas import tpu as pltpu
from jax.sharding import PartitionSpec as P

MESH = pl.DeviceIdType.MESH
HIGH = lax.Precision.HIGHEST
F32 = jnp.float32
BF16 = jnp.bfloat16

RING = 16
HALF = 64
RANK = 64
PARTS = 4
ROWS = 128 // PARTS


ORDER = (
    "s_near start_x start_g t_zero f_make t_one x1 t_three s_far x2 f_send_out t_four x3 "
    "g_ym g_yp g_xp p_xp x4 f_sum s_row x5 g_y2 x6 f_end x7 s_end x8 g_rest p_make "
    "g_last c_one c_two t_five c_three c_four"
)


def dot(a, b, dims, precision=None):
    return lax.dot_general(a, b, (dims, ((), ())), precision=precision, preferred_element_type=F32)


def kernel(
    x_ref, g_ref, e_ref, bt_ref,
    comp_hbm, ortho_ref, basis_ref,
    xg, gg, acc, xt, comp_ref, e_in, bt, s_one, s_two, f_out, f_in, f_own, f_all, s_all, p_mine, p_peer,
    gram_mine, gram_all, mat, u_out, u_in, u_own, u_all,
    loc_sem, x_send, xr_recv, xl_recv, g_send, g_recv, d_send, d_recv,
    s_send, s_recv, f_send, f_recv, r_send, r_recv, p_send, p_recv, gr_send, gr_recv, u_send, u_recv, near,
):
    row, col, rep = lax.axis_index("row"), lax.axis_index("col"), lax.axis_index("rep")
    y, x, core = row // 4, (row // 2) % 2, row % 2

    def at_row(yy, xx, cc):
        return lax.rem(yy + 4, 4) * 4 + xx * 2 + cc

    def wrap(v):
        return lax.rem(v + RING, RING)

    def place_of(dy, dx):
        return dy + dy // 2 - 2 * (dy // 3) + 4 * dx

    def remote(src, dst, ssem, rsem, where):
        return pltpu.make_async_remote_copy(
            src_ref=src, dst_ref=dst, send_sem=ssem, recv_sem=rsem,
            device_id=where, device_id_type=MESH,
        )

    here = (row, col, 1 - rep)
    sends = []

    def send(src, dst, ssem, rsem, where):
        copy = remote(src, dst, ssem, rsem, where)
        copy.start()
        sends.append(copy)

    def arrived(dst, rsem):
        remote(dst, dst, rsem, rsem, here).wait_recv()

    def sent(src, ssem):
        remote(src, src, ssem, ssem, here).wait_send()

    own_g = pltpu.make_async_copy(g_ref, gg.at[pl.ds(0, 2)], loc_sem.at[0])
    own_b = pltpu.make_async_copy(bt_ref, bt, loc_sem.at[1])
    own_x = pltpu.make_async_copy(x_ref, xg.at[pl.ds(PARTS * col, PARTS)], loc_sem.at[2])
    own_e = pltpu.make_async_copy(e_ref.at[0], e_in, loc_sem.at[3])
    for copy in (own_g, own_b, own_x, own_e):
        copy.start()

    barrier = pltpu.get_barrier_semaphore()

    def signal(where):
        pl.semaphore_signal(barrier, inc=1, device_id=where, device_id_type=MESH)

    right, left = (row, wrap(col + 1), rep), (row, wrap(col - 1), rep)
    up, down, side, sib = (
        (at_row(y + 1, x, core), col, rep),
        (at_row(y - 1, x, core), col, rep),
        (at_row(y, 1 - x, core), col, rep),
        (at_row(y, x, 1 - core), col, rep),
    )
    for where in (right, left, up, down, side, sib, here):
        signal(where)
    for k in (2, 3):
        signal((row, wrap(col + k), rep))
        signal((row, wrap(col - k), rep))

    def tell(k, *to):
        for where in to:
            pl.semaphore_signal(near.at[k], inc=1, device_id=where, device_id_type=MESH)

    def told(k, count):
        pl.semaphore_wait(near.at[k], count)

    own_g.wait()
    own_b.wait()
    quarter, group = lax.rem(col, 4), col // 4
    s_one[quarter] = dot(bt[...], gg[0:2].reshape(128, 1536), ((1,), (1,))).astype(BF16)
    own_x.wait()

    pl.semaphore_wait(barrier, 11)
    plane = (up, down, side, sib)

    def x_part(owner, part):
        return xg.at[PARTS * owner + part]

    def x_push(owner, part, k, side):
        ref = x_part(owner, part)
        recv = (xr_recv if side == 0 else xl_recv).at[PARTS * k + part]
        remote(ref, ref, x_send.at[side], recv, right if side == 0 else left).start()

    def x_turn(owner):
        slot = 2 * place_of(lax.rem(owner // 4 - y + 4, 4), lax.rem(owner // 2 + x, 2)) + lax.rem(owner + core, 2)
        xt[:, pl.ds(pl.multiple_of(slot * 128, 128), 128)] = xg[pl.ds(PARTS * owner, PARTS)].reshape(128, 384).T

    def x_step(k):
        frm, to = wrap(col - k), wrap(col + k)
        for i in range(PARTS):
            if k < 8 or i < PARTS // 2:
                arrived(x_part(frm, i), xr_recv.at[PARTS * (k - 1) + i])
                if k < 7 or (k == 7 and i < PARTS // 2):
                    x_push(frm, i, k, 0)
            i = PARTS - 1 - i
            if k < 8 or i >= PARTS // 2:
                arrived(x_part(to, i), xl_recv.at[PARTS * (k - 1) + i])
                if k < 7 or (k == 7 and i >= PARTS // 2):
                    x_push(to, i, k, 1)
        x_turn(frm)
        if k < 8:
            x_turn(to)

    OWN, YP, YM, Y2, XP, YPX, YMX, Y2X = range(8)
    FIRST, SECOND, WHOLE = (0, 1), (1, 1), (0, 2)

    def block(name, part, other=0):
        return gg.at[pl.ds(2 * (2 * name + other) + part[0], part[1])]

    def push(src, k, dst, where, part=WHOLE):
        remote(block(src, part), block(dst, part), g_send, g_recv.at[k], where).start()

    def got(k, name, part=WHOLE):
        arrived(block(name, part), g_recv.at[k])
        share(k, name, part)

    def share(k, name, part=WHOLE):
        remote(block(name, part), block(name, part, 1), d_send, d_recv.at[k], sib).start()

    def shared(k, name, part=WHOLE):
        arrived(block(name, part, 1), d_recv.at[k])

    def start_x():
        for part in range(PARTS):
            x_push(col, part, 0, 0)
            x_push(col, PARTS - 1 - part, 0, 1)
        x_turn(col)

    def start_g():
        push(OWN, 0, XP, side)
        push(OWN, 1, YM, up)
        push(OWN, 2, YP, down)
        share(9, OWN)

    def g_ym():
        got(1, YM)
        push(YM, 3, Y2, up, FIRST)

    def g_yp():
        got(2, YP)
        push(YP, 4, Y2, down, SECOND)

    def g_xp():
        got(0, XP)

    def p_xp():
        push(XP, 5, YMX, up)
        push(XP, 6, YPX, down)

    def g_y2():
        got(3, Y2, FIRST)
        push(Y2, 7, Y2X, side, FIRST)
        got(4, Y2, SECOND)
        push(Y2, 8, Y2X, side, SECOND)

    f_owner = quarter > 0
    f_count = 12

    def f_make():
        own_e.wait()
        ft = dot(bt[...], e_in[...], ((1,), (1,))).astype(BF16)
        for a in range(4):
            for b in range(3):
                f_out[4 * a + b + 1] = ft[16 * a:16 * a + 16, 128 * b:128 * b + 128]

    def f_send_out():
        @pl.loop(1, RING)
        def _(k):
            to = wrap(col + k)

            @pl.when(lax.rem(to, 4) > 0)
            def _():
                remote(f_out.at[to], f_in.at[col], f_send.at[0], f_recv.at[0], (row, to, rep)).start()

    def f_sum():
        @pl.when(f_owner)
        def _():
            f_in[col] = f_out[col]
            arrived(f_in.at[pl.ds(0, RING - 1)], f_recv.at[0])
            f_own[...] = jnp.sum(f_in[...].astype(F32), axis=0).astype(BF16)

            @pl.loop(1, RING)
            def _(k):
                remote(f_own, f_all.at[col], f_send.at[1], f_recv.at[1], (row, wrap(col + k), rep)).start()

            f_all[col] = f_own[...]
            sent(f_out.at[pl.ds(0, f_count - 1)], f_send.at[0])

    def f_end():
        @pl.when(f_owner)
        def _():
            arrived(f_all.at[pl.ds(0, f_count - 1)], f_recv.at[1])
            sent(f_in.at[pl.ds(0, RING - 1)], f_send.at[1])

        @pl.when(jnp.logical_not(f_owner))
        def _():
            arrived(f_all.at[pl.ds(0, f_count)], f_recv.at[1])
            sent(f_out.at[pl.ds(0, f_count)], f_send.at[0])

    def s_near():
        for k in range(1, 4):
            to = lax.rem(quarter + k, 4)
            send(s_one.at[quarter], s_one.at[quarter], s_send.at[0, k], s_recv.at[0, k], (row, group * 4 + to, rep))

    def s_far():
        for k in range(1, 4):
            arrived(s_one.at[lax.rem(quarter + 4 - k, 4)], s_recv.at[0, k])
        s_two[group] = jnp.sum(s_one[...].astype(F32), axis=0).astype(BF16)
        for k in range(1, 4):
            to = lax.rem(group + k, 4)
            send(s_two.at[group], s_two.at[group], s_send.at[1, k], s_recv.at[1, k], (row, to * 4 + quarter, rep))

    def s_row():
        for k in range(1, 4):
            arrived(s_two.at[lax.rem(group + 4 - k, 4)], s_recv.at[1, k])
        s_all[row] = jnp.sum(s_two[...].astype(F32), axis=0).astype(BF16)

        @pl.loop(1, RING)
        def _(k):
            remote(s_all.at[row], s_all.at[row], r_send.at[0], r_recv.at[0], (wrap(row + k), col, rep)).start()

    def s_end():
        arrived(s_all.at[pl.ds(0, RING - 1)], r_recv.at[0])

    def p_make():
        s_wide = jnp.concatenate([s_all[t] for t in range(RING)], axis=1)
        f_wide = jnp.concatenate(
            [jnp.concatenate([f_all[4 * a + b + 1] for a in range(4)], axis=0) for b in range(3)],
            axis=1,
        )
        p_part = dot(s_wide, xg[...].reshape(RING * 128, 384), ((1,), (0,)))
        p_mine[...] = (p_part + f_wide.astype(F32)).astype(BF16)
        send(p_mine, p_peer, p_send, p_recv, (row, col, 1 - rep))

    def multiply(first, count, base, out):
        ks = slice(256 * first, 256 * (first + count))

        @pl.loop(0, 3)
        def _(n):
            cols = pl.ds(pl.multiple_of(n * 512, 512), 512)
            gs = gg[4 * first:4 * (first + count), :, cols].reshape(256 * count, 512)
            out[:, cols] = (base[:, cols].astype(F32) + dot(xt[:, ks], gs, ((1,), (0,)))).astype(out.dtype)

    def c_one():
        shared(9, OWN)
        shared(1, YM)
        shared(2, YP)
        multiply(OWN, 3, e_in, acc)

    def c_two():
        shared(0, XP)
        shared(3, Y2, FIRST)
        shared(4, Y2, SECOND)
        multiply(Y2, 2, acc, acc)

    def g_rest():
        got(5, YMX)
        got(6, YPX)

    def g_last():
        got(7, Y2X, FIRST)
        got(8, Y2X, SECOND)

    def c_three():
        shared(5, YMX)
        shared(6, YPX)
        multiply(YPX, 2, acc, acc)

    def c_four():
        shared(7, Y2X, FIRST)
        shared(8, Y2X, SECOND)
        multiply(Y2X, 1, acc, comp_ref)

    def t_zero():
        tell(0, right, left)
        tell(3, *plane)

    def t_one():
        told(0, 2)
        tell(1, (row, wrap(col + 4), rep), (row, wrap(col - 4), rep))
        told(3, 4)
        tell(4, *plane)

    def t_three():
        told(1, 2)
        told(4, 4)
        tell(5, *plane)

    def t_four():
        told(5, 4)
        tell(6, here)

    def t_five():
        told(6, 1)

    steps = {f.__name__: f for f in (
        start_x, start_g, t_zero, f_make, t_one, s_near, t_three, f_send_out, s_far, t_four, g_ym,
        g_yp, g_xp, p_xp, f_sum, s_row, g_y2, f_end, s_end, p_make, c_one, g_rest, c_two, t_five, g_last, c_three, c_four,
    )}
    steps.update({"x%d" % k: functools.partial(x_step, k) for k in range(1, 9)})
    for name in ORDER.split():
        steps[name]()
    arrived(p_peer, p_recv)
    p_t = (p_mine[...].astype(F32) + p_peer[...].astype(F32)) * 0.5

    comp_out = pltpu.make_async_copy(comp_ref, comp_hbm, loc_sem.at[0])
    comp_out.start()

    p_high = p_t.astype(BF16)
    p_rest = (p_t - p_high.astype(F32)).astype(BF16)
    p_both = jnp.concatenate([p_high, p_rest], axis=0)
    me = row + RING * rep
    mine = row // 2 + 8 * rep
    owner = core == x

    def piece_at(k):
        chip = lax.rem(k, 8)
        return (2 * chip + lax.rem(chip, 2), col, k // 8)

    for b in range(4):
        cols = slice(384 * b, 384 * b + 384)
        ut = dot(p_both, comp_ref[:, cols], ((1,), (0,)))
        ut = (ut[:RANK] + ut[RANK:]).astype(BF16)
        for a in range(4):
            u_out[4 * a + b] = ut[16 * a:16 * a + 16, :]

    @pl.loop(0, RING)
    def _(k):
        @pl.when(jnp.logical_not(jnp.logical_and(owner, k == mine)))
        def _():
            remote(u_out.at[k], u_in.at[me], u_send.at[0], u_recv.at[0], piece_at(k)).start()

    gram = dot(p_t, p_t, ((1,), (1,)), HIGH)
    gram_mine[...] = jnp.concatenate([gram[:32], gram[32:]], axis=1)

    @pl.loop(1, RING)
    def _(k):
        to = wrap(row + k)
        remote(gram_mine, gram_all.at[row], gr_send, gr_recv, (to, col, rep)).start()

    gram_all[row] = gram_mine[...]

    @pl.when(owner)
    def _():
        u_in[me] = u_out[mine]
        arrived(u_in.at[pl.ds(0, 31)], u_recv.at[0])
        u_own[...] = jnp.sum(u_in[...].astype(F32), axis=0).astype(BF16)

        for dy in (2, 3, 1, 0):
            base = lax.rem(y + dy, 4) * 4

            @pl.loop(0, 8)
            def _(k):
                to = base + lax.rem(k, 4)

                def go():
                    remote(u_own, u_all.at[mine], u_send.at[1], u_recv.at[1], (to, col, k // 4)).start()

                if dy:
                    go()
                else:
                    pl.when(to + RING * (k // 4) != me)(go)

        u_all[mine] = u_own[...]

    arrived(gram_all.at[pl.ds(0, RING - 1)], gr_recv)
    total = jnp.sum(gram_all[...], axis=0)
    gram = jnp.concatenate([total[:, :RANK], total[:, RANK:]], axis=0)
    subl = lax.broadcasted_iota(jnp.int32, (RANK, 128), 0)
    lane = lax.broadcasted_iota(jnp.int32, (RANK, 128), 1)
    mat[...] = jnp.concatenate([gram, (subl == lane)[:, :RANK].astype(F32)], axis=1)

    def pick(rows, k):
        return jnp.sum(jnp.where(lane[:rows.shape[0]] == k, rows, 0.0), axis=1, keepdims=True)

    def eliminate(h, carry):
        k = 2 * h
        m = mat[...]
        row_a, row_b = mat[pl.ds(k, 1), :], mat[pl.ds(k + 1, 1), :]
        col_a, col_b = pick(m, k), pick(m, k + 1)
        corner, cross = pick(row_a, k), pick(row_a, k + 1)
        below, last = pick(row_b, k), pick(row_b, k + 1)
        inverse = 1.0 / corner
        step = below * inverse
        row_b = row_b - step * row_a
        factor_a = col_a * inverse
        factor_b = (col_b - factor_a * cross) / (last - step * cross)
        factor_a = jnp.where(subl[:, :1] > k, factor_a, 0.0)
        factor_b = jnp.where(subl[:, :1] > k + 1, factor_b, 0.0)
        mat[...] = m - factor_a * row_a - factor_b * row_b
        return carry

    lax.fori_loop(0, RANK // 2, eliminate, 0)
    d = jnp.sum(jnp.where(lane == subl, mat[...], 0.0), axis=1, keepdims=True)
    inv_factor = lax.rsqrt(d) * mat[:, RANK:]
    ortho_ref[...] = dot(inv_factor, p_t, ((1,), (0,)), HIGH).astype(BF16)

    @pl.when(owner)
    def _():
        arrived(u_all.at[pl.ds(0, 15)], u_recv.at[1])
        sent(u_out.at[pl.ds(0, 15)], u_send.at[0])
        sent(u_in.at[pl.ds(0, 31)], u_send.at[1])

    @pl.when(jnp.logical_not(owner))
    def _():
        arrived(u_all, u_recv.at[1])
        sent(u_out, u_send.at[0])

    for b in range(4):
        ut = jnp.concatenate([u_all[4 * a + b] for a in range(4)], axis=0).astype(F32) * 0.5
        basis_ref[:, 384 * b:384 * b + 384] = dot(inv_factor, ut, ((1,), (0,)), HIGH)

    comp_out.wait()
    for copy in sends:
        copy.wait_send()
    for k in range(2):
        sent(xg.at[pl.ds(0, 7 * PARTS + PARTS // 2)], x_send.at[k])
    sent(gg.at[pl.ds(0, 14)], g_send)
    sent(gg.at[pl.ds(0, 16)], d_send)
    sent(s_all.at[pl.ds(0, 15)], r_send.at[0])
    sent(gram_all.at[pl.ds(0, 15)], gr_send)


def body(layer_inputs, output_grads, error_prev, basis_prev):
    dma = pltpu.SemaphoreType.DMA
    vmem = pltpu.VMEM
    comp, ortho_t, basis_t = pl.pallas_call(
        kernel,
        out_shape=(
            jax.ShapeDtypeStruct((384, 1536), BF16),
            jax.ShapeDtypeStruct((RANK, 384), BF16),
            jax.ShapeDtypeStruct((RANK, 1536), F32),
        ),
        in_specs=[pl.BlockSpec(memory_space=pl.ANY)] * 4,
        out_specs=[pl.BlockSpec(memory_space=pl.ANY)] + [pl.BlockSpec(memory_space=vmem)] * 2,
        scratch_shapes=[
            vmem((16 * PARTS, ROWS, 384), BF16),
            vmem((32, HALF, 1536), BF16),
            vmem((384, 1536), F32),
            vmem((384, 2048), BF16),
            vmem((384, 1536), BF16),
            vmem((384, 1536), BF16),
            vmem((RANK, 1536), BF16),
            vmem((4, RANK, 128), BF16),
            vmem((4, RANK, 128), BF16),
            vmem((16, 16, 128), BF16),
            vmem((16, 16, 128), BF16),
            vmem((16, 128), BF16),
            vmem((16, 16, 128), BF16),
            vmem((16, RANK, 128), BF16),
            vmem((RANK, 384), BF16),
            vmem((RANK, 384), BF16),
            vmem((32, 128), F32),
            vmem((16, 32, 128), F32),
            vmem((RANK, 128), F32),
            vmem((16, 16, 384), BF16),
            vmem((32, 16, 384), BF16),
            vmem((16, 384), BF16),
            vmem((16, 16, 384), BF16),
            dma((4,)),
            dma((2,)), dma((8 * PARTS,)), dma((8 * PARTS,)),
            dma(()), dma((9,)), dma(()), dma((10,)),
            dma((2, 4)), dma((2, 4)), dma((2,)), dma((2,)), dma((1,)), dma((1,)),
            dma(()), dma(()), dma(()), dma(()), dma((2,)), dma((2,)),
            pltpu.SemaphoreType.REGULAR((7,)),
        ],
        compiler_params=pltpu.CompilerParams(
            collective_id=0, has_side_effects=True, vmem_limit_bytes=60 * 2**20
        ),
        name="powersgd",
    )(layer_inputs.reshape(PARTS, ROWS, 384), output_grads.reshape(2, HALF, 1536), error_prev, basis_prev.T)
    basis_next = basis_t.T
    approx = dot(ortho_t, basis_t.astype(BF16), ((0,), (0,)))
    error_next = (comp.astype(F32) - approx).astype(BF16)
    return (basis_next, error_next[None])


def solution(mesh):
    return jax.shard_map(
        body,
        mesh=mesh,
        in_specs=(
            P("rep", "col", "row"),
            P("rep", "row", "col"),
            P("rep", "row", "col"),
            P("col", None),
        ),
        out_specs=(P("col", None), P("rep", "row", "col")),
        check_vma=False,
    )
```

time: 78.3 us -> 69.7 us (0.89)
  Pallas kernels: 73.8 us -> 65.1 us
    pallas_call x1, Pallas kernels: 73.8 us -> 65.1 us  [body(): pl.pallas_call(kernel, out_shape=(jax.ShapeDtypeStruct((384, 1536), BF16)...]
where the time goes in v3:
time: 69.7 us; the launch traced here: 69.5 us
  Pallas kernels  65.1 us (93%)
  matrix products  2.97 us (4%)
  local copies, waits for them, and re-layouts  0.75 us (1%)
    pallas_call x1, Pallas kernels, body(): pl.pallas_call(kernel, out_shape=(jax.ShapeDtypeStruct((384, 1536), BF16)...  65.1 us
    dot_general x1, matrix products, dot(): lax.dot_general(a, b, (dims, ((), ())), precision=precision, preferred_el...  2.97 us

profile of v3, /device:TPU:1, one launch (start us, length us, event | category | flops | bytes accessed | tf_op | source)
XLA Modules:
  0.0 69.5 jit_solution(4576388724538315910)
XLA Ops:
  0.6 65.1 %powersgd.1 = (bf16[384,1536]{1,0:T(8,128)(2,1)}, bf16[64,384]{1,0:T(8,128)(2,1)}, f32[64,1536]{1,0:T(8,128)}) custom-call(bf16[4,32,384]{2,1,0:T(8,128)(2,1)} %bitcast.10, bf16[2,64,1536]{2,1,0:T(8,128)(2,1)} %bitcast.8, bf16[1,384,1536]{2,1,0:T(8,128)(2,1)} %e_ref.1, bf16[64,1536]{1,0:T(8,128)(2,1)} %bitcast.9), custom_call_target="tpu_custom_call" | custom-call | tf_op jit(solution)/shard_map/powersgd/pallas_call | solution.py:465
  65.8 0.0 copy-start
  65.8 3.0 %fusion.1 = bf16[1,384,1536]{2,1,0:T(8,128)(2,1)} fusion(bf16[64,384]{1,0:T(8,128)(2,1)} %get-tuple-element.7, bf16[384,1536]{1,0:T(8,128)(2,1)} %get-tuple-element.6, f32[64,1536]{1,0:T(8,128)} %get-tuple-element.5), kind=kOutput, calls=%fused_computation.2 | convolution fusion | flops 77365248 | bytes 2801664 | tf_op jit(solution)/shard_map/dot_general | solution.py:30
  68.8 0.0 copy-done
  68.8 0.7 %copy.7 = f32[1536,64]{0,1:T(8,128)} copy(f32[1536,64]{0,1:T(8,128)S(1)} %bitcast.7) | data formatting | bytes 786432
Async XLA Ops:
  65.8 3.0 %copy-start = (f32[64,1536]{1,0:T(8,128)S(1)}, f32[64,1536]{1,0:T(8,128)}, u32[]{:S(2)}) copy-start(f32[64,1536]{1,0:T(8,128)} %get-tuple-element.5) | copy-start | bytes 1179652

commit v4 on v3

--- a/solution.py
+++ b/solution.py
@@ -21,7 +21,7 @@
 
 ORDER = (
     "s_near start_x start_g t_zero f_make t_one x1 t_three s_far x2 f_send_out t_four x3 "
-    "g_ym g_yp g_xp p_xp x4 f_sum s_row x5 g_y2 x6 f_end x7 s_end x8 g_rest p_make "
+    "g_ym g_yp g_xp p_xp x4 f_sum s_row x5 g_y2 x6 f_end x7 g_rest s_end x8 p_make "
     "g_last c_one c_two t_five c_three c_four"
 )
 

time: 69.7 us -> 68.8 us (0.987)
  Pallas kernels: 65.1 us -> 64.3 us
    pallas_call x1, Pallas kernels: 65.1 us -> 64.3 us  [body(): pl.pallas_call(kernel, out_shape=(jax.ShapeDtypeStruct((384, 1536), BF16)...]
where the time goes in v4:
time: 68.8 us; the launch traced here: 68.6 us
  Pallas kernels  64.3 us (93%)
  matrix products  2.97 us (4%)
  local copies, waits for them, and re-layouts  0.75 us (1%)
    pallas_call x1, Pallas kernels, body(): pl.pallas_call(kernel, out_shape=(jax.ShapeDtypeStruct((384, 1536), BF16)...  64.3 us
    dot_general x1, matrix products, dot(): lax.dot_general(a, b, (dims, ((), ())), precision=precision, preferred_el...  2.97 us

profile of v4, /device:TPU:1, one launch (start us, length us, event | category | flops | bytes accessed | tf_op | source)
XLA Modules:
  0.0 68.6 jit_solution(11944631298368930964)
XLA Ops:
  0.6 64.3 %powersgd.1 = (bf16[384,1536]{1,0:T(8,128)(2,1)}, bf16[64,384]{1,0:T(8,128)(2,1)}, f32[64,1536]{1,0:T(8,128)}) custom-call(bf16[4,32,384]{2,1,0:T(8,128)(2,1)} %bitcast.10, bf16[2,64,1536]{2,1,0:T(8,128)(2,1)} %bitcast.8, bf16[1,384,1536]{2,1,0:T(8,128)(2,1)} %e_ref.1, bf16[64,1536]{1,0:T(8,128)(2,1)} %bitcast.9), custom_call_target="tpu_custom_call" | custom-call | tf_op jit(solution)/shard_map/powersgd/pallas_call | solution.py:465
  64.9 0.0 copy-start
  64.9 3.0 %fusion.1 = bf16[1,384,1536]{2,1,0:T(8,128)(2,1)} fusion(bf16[64,384]{1,0:T(8,128)(2,1)} %get-tuple-element.7, bf16[384,1536]{1,0:T(8,128)(2,1)} %get-tuple-element.6, f32[64,1536]{1,0:T(8,128)} %get-tuple-element.5), kind=kOutput, calls=%fused_computation.2 | convolution fusion | flops 77365248 | bytes 2801664 | tf_op jit(solution)/shard_map/dot_general | solution.py:30
  67.9 0.0 copy-done
  67.9 0.7 %copy.7 = f32[1536,64]{0,1:T(8,128)} copy(f32[1536,64]{0,1:T(8,128)S(1)} %bitcast.7) | data formatting | bytes 786432
Async XLA Ops:
  64.9 3.0 %copy-start = (f32[64,1536]{1,0:T(8,128)S(1)}, f32[64,1536]{1,0:T(8,128)}, u32[]{:S(2)}) copy-start(f32[64,1536]{1,0:T(8,128)} %get-tuple-element.5) | copy-start | bytes 1179652

commit v5 on v4

--- a/solution.py
+++ b/solution.py
@@ -1,5 +1,3 @@
-import functools
-
 import jax
 import jax.numpy as jnp
 from jax import lax
@@ -17,13 +15,6 @@
 RANK = 64
 PARTS = 4
 ROWS = 128 // PARTS
-
-
-ORDER = (
-    "s_near start_x start_g t_zero f_make t_one x1 t_three s_far x2 f_send_out t_four x3 "
-    "g_ym g_yp g_xp p_xp x4 f_sum s_row x5 g_y2 x6 f_end x7 g_rest s_end x8 p_make "
-    "g_last c_one c_two t_five c_three c_four"
-)
 
 
 def dot(a, b, dims, precision=None):
@@ -331,13 +322,41 @@
     def t_five():
         told(6, 1)
 
-    steps = {f.__name__: f for f in (
-        start_x, start_g, t_zero, f_make, t_one, s_near, t_three, f_send_out, s_far, t_four, g_ym,
-        g_yp, g_xp, p_xp, f_sum, s_row, g_y2, f_end, s_end, p_make, c_one, g_rest, c_two, t_five, g_last, c_three, c_four,
-    )}
-    steps.update({"x%d" % k: functools.partial(x_step, k) for k in range(1, 9)})
-    for name in ORDER.split():
-        steps[name]()
+    s_near()
+    start_x()
+    start_g()
+    t_zero()
+    f_make()
+    t_one()
+    x_step(1)
+    t_three()
+    s_far()
+    x_step(2)
+    f_send_out()
+    t_four()
+    x_step(3)
+    g_ym()
+    g_yp()
+    g_xp()
+    p_xp()
+    x_step(4)
+    f_sum()
+    s_row()
+    x_step(5)
+    g_y2()
+    x_step(6)
+    f_end()
+    x_step(7)
+    g_rest()
+    s_end()
+    x_step(8)
+    p_make()
+    g_last()
+    c_one()
+    c_two()
+    t_five()
+    c_three()
+    c_four()
     arrived(p_peer, p_recv)
     p_t = (p_mine[...].astype(F32) + p_peer[...].astype(F32)) * 0.5
 

time: 68.8 us -> 68.8 us (level)
  no operation moved by 1% of the time
where the time goes in v5:
time: 68.8 us; the launch traced here: 68.6 us
  Pallas kernels  64.3 us (93%)
  matrix products  2.97 us (4%)
  local copies, waits for them, and re-layouts  0.75 us (1%)
    pallas_call x1, Pallas kernels, body(): pl.pallas_call(kernel, out_shape=(jax.ShapeDtypeStruct((384, 1536), BF16)...  64.3 us
    dot_general x1, matrix products, dot(): lax.dot_general(a, b, (dims, ((), ())), precision=precision, preferred_el...  2.97 us

profile of v5, /device:TPU:1, one launch (start us, length us, event | category | flops | bytes accessed | tf_op | source)
XLA Modules:
  0.0 68.6 jit_solution(11944631298368930964)
XLA Ops:
  0.6 64.3 %powersgd.1 = (bf16[384,1536]{1,0:T(8,128)(2,1)}, bf16[64,384]{1,0:T(8,128)(2,1)}, f32[64,1536]{1,0:T(8,128)}) custom-call(bf16[4,32,384]{2,1,0:T(8,128)(2,1)} %bitcast.10, bf16[2,64,1536]{2,1,0:T(8,128)(2,1)} %bitcast.8, bf16[1,384,1536]{2,1,0:T(8,128)(2,1)} %e_ref.1, bf16[64,1536]{1,0:T(8,128)(2,1)} %bitcast.9), custom_call_target="tpu_custom_call" | custom-call | tf_op jit(solution)/shard_map/powersgd/pallas_call | solution.py:484
  64.9 0.0 copy-start
  64.9 3.0 %fusion.1 = bf16[1,384,1536]{2,1,0:T(8,128)(2,1)} fusion(bf16[64,384]{1,0:T(8,128)(2,1)} %get-tuple-element.7, bf16[384,1536]{1,0:T(8,128)(2,1)} %get-tuple-element.6, f32[64,1536]{1,0:T(8,128)} %get-tuple-element.5), kind=kOutput, calls=%fused_computation.2 | convolution fusion | flops 77365248 | bytes 2801664 | tf_op jit(solution)/shard_map/dot_general | solution.py:21
  67.9 0.0 copy-done
  67.9 0.7 %copy.7 = f32[1536,64]{0,1:T(8,128)} copy(f32[1536,64]{0,1:T(8,128)S(1)} %bitcast.7) | data formatting | bytes 786432
Async XLA Ops:
  64.9 3.0 %copy-start = (f32[64,1536]{1,0:T(8,128)S(1)}, f32[64,1536]{1,0:T(8,128)}, u32[]{:S(2)}) copy-start(f32[64,1536]{1,0:T(8,128)} %get-tuple-element.5) | copy-start | bytes 1179652

commit v6 on v5

--- a/solution.py
+++ b/solution.py
@@ -126,8 +126,8 @@
                 arrived(x_part(to, i), xl_recv.at[PARTS * (k - 1) + i])
                 if k < 7 or (k == 7 and i >= PARTS // 2):
                     x_push(to, i, k, 1)
-        x_turn(frm)
-        if k < 8:
+        if k < 7:
+            x_turn(frm)
             x_turn(to)
 
     OWN, YP, YM, Y2, XP, YPX, YMX, Y2X = range(8)
@@ -351,6 +351,8 @@
     s_end()
     x_step(8)
     p_make()
+    for k in (7, 8, 9):
+        x_turn(wrap(col + k))
     g_last()
     c_one()
     c_two()

time: 68.8 us -> 68.9 us (level)
  no operation moved by 1% of the time
where the time goes in v6:
time: 68.9 us; the launch traced here: 68.7 us
  Pallas kernels  64.4 us (93%)
  matrix products  2.97 us (4%)
  local copies, waits for them, and re-layouts  0.75 us (1%)
    pallas_call x1, Pallas kernels, body(): pl.pallas_call(kernel, out_shape=(jax.ShapeDtypeStruct((384, 1536), BF16)...  64.4 us
    dot_general x1, matrix products, dot(): lax.dot_general(a, b, (dims, ((), ())), precision=precision, preferred_el...  2.97 us

profile of v6, /device:TPU:1, one launch (start us, length us, event | category | flops | bytes accessed | tf_op | source)
XLA Modules:
  0.0 68.7 jit_solution(10501433836995315125)
XLA Ops:
  0.6 64.4 %powersgd.1 = (bf16[384,1536]{1,0:T(8,128)(2,1)}, bf16[64,384]{1,0:T(8,128)(2,1)}, f32[64,1536]{1,0:T(8,128)}) custom-call(bf16[4,32,384]{2,1,0:T(8,128)(2,1)} %bitcast.10, bf16[2,64,1536]{2,1,0:T(8,128)(2,1)} %bitcast.8, bf16[1,384,1536]{2,1,0:T(8,128)(2,1)} %e_ref.1, bf16[64,1536]{1,0:T(8,128)(2,1)} %bitcast.9), custom_call_target="tpu_custom_call" | custom-call | tf_op jit(solution)/shard_map/powersgd/pallas_call | solution.py:486
  65.0 0.0 copy-start
  65.0 3.0 %fusion.1 = bf16[1,384,1536]{2,1,0:T(8,128)(2,1)} fusion(bf16[64,384]{1,0:T(8,128)(2,1)} %get-tuple-element.7, bf16[384,1536]{1,0:T(8,128)(2,1)} %get-tuple-element.6, f32[64,1536]{1,0:T(8,128)} %get-tuple-element.5), kind=kOutput, calls=%fused_computation.2 | convolution fusion | flops 77365248 | bytes 2801664 | tf_op jit(solution)/shard_map/dot_general | solution.py:21
  68.0 0.0 copy-done
  68.0 0.7 %copy.7 = f32[1536,64]{0,1:T(8,128)} copy(f32[1536,64]{0,1:T(8,128)S(1)} %bitcast.7) | data formatting | bytes 786432
Async XLA Ops:
  65.0 3.0 %copy-start = (f32[64,1536]{1,0:T(8,128)S(1)}, f32[64,1536]{1,0:T(8,128)}, u32[]{:S(2)}) copy-start(f32[64,1536]{1,0:T(8,128)} %get-tuple-element.5) | copy-start | bytes 1179652
